TPU v7x, 32 devices: a whole 2x2x4 slice. The times are simulated.
32 devices in a mesh: grp: 2 (over y), ctx: 4 (over z), hd: 2 (over x), pf: 2 (over core).
Axes of the slice: x: 2, y: 2, z: 4, core: 2. Of those that a mesh axis runs over, the one named last changes fastest.
Arguments:
- latent_pages: bfloat16 [256, 16, 16, 512], P(('ctx', 'hd', 'pf'), 'grp'), parts along dimension 1, may hold values from -6 to 6
- page_target: int32 [256, 16, 1], P(None, 'grp'), parts along dimension 1, may hold values from 0 to 3; in each aligned block of 128 rows (0 to 127, 128 to 255, ..., all dimensions but the last counted through in order) at most 36 rows name the same one
- page_count: int32 [256, 16], P(None, 'grp'), parts along dimension 1, may hold values from 1 to 16
- context_length: int32 [16], P('grp'), parts along dimension 0, may hold values from 1024 to 4094
- queries: bfloat16 [2, 16, 8192], P(None, 'grp', 'hd'), parts along dimension 1, may hold values from -110 to 110
- key_up: bfloat16 [256, 1024], replicated, may hold values from -0.375 to 0.375
- value_up: bfloat16 [256, 1024], P(None, 'hd'), may hold values from -2.5 to 2.5
Outputs:
- attended: bfloat16 [2, 16, 8192], P(None, 'grp', 'hd'), parts along dimension 1
- stored_pages: bfloat16 [4608, 16, 512], P(('grp', 'ctx', 'hd', 'pf')), parts along dimension 0
There are 2 independent parts, one for each index of `grp`. A program takes and returns all parts, laid end to end along the dimension named above; an argument that names none is the same for every part. Nothing has to cross between parts.
Inputs may be any that keep to these rules, and one draw needn't show every extreme that they name: `page_target`: among the 128 rows of one sending device (pages d*16 to (d+1)*16 - 1, every request), no value appears more than 36 times.
All inputs are finite; a program needn't handle non-finite values.
Results may differ from a plain program's by a relative error of at most 0.02.
The roundings to bfloat16 on the way count: a program that leaves them out, or rounds other values in their place, can miss the bound.
Values may be sent and summed in bfloat16 or wider, within the bound.
A program may use at most 128 MiB of HBM per device.

v0:
```python
import math

import jax
import jax.numpy as jnp
from jax import lax
from jax.sharding import PartitionSpec as P

KVH = 8
GROUP = 8
HD_DIM = 128
LATK = 256
LATV = 256
PAGE = 16
STEPS = 2
REQS = 8


def frequencies(head_width):
    exponent = jnp.arange(0, head_width, 2).astype(jnp.float32) / head_width
    inverse = jnp.power(jnp.float32(500000.0), -exponent)
    wavelength = 2.0 * math.pi / inverse
    smooth = (8192.0 / wavelength - 1.0) / 3.0
    mixed = (1.0 - smooth) * inverse / 8.0 + smooth * inverse
    return jnp.where(
        wavelength > 8192.0, inverse / 8.0, jnp.where(wavelength < 2048.0, inverse, mixed)
    )


def rotate(values, position):
    halfway = values.shape[-1] // 2
    angles = position[..., None] * frequencies(values.shape[-1])
    cosine = jnp.cos(angles)
    sine_part = jnp.sin(angles)
    first_half = values[..., :halfway]
    second_half = values[..., halfway:]
    return jnp.concatenate(
        [
            first_half * cosine - second_half * sine_part,
            second_half * cosine + first_half * sine_part,
        ],
        axis=-1,
    )


def on_device(latent_pages, page_target, page_count, context_length, queries, key_up, value_up):
    context_devices = lax.axis_size("ctx")
    head_devices = lax.axis_size("hd")
    core_devices = lax.axis_size("pf")
    lane_count = head_devices * core_devices
    lane_index = lax.axis_index("hd") * core_devices + lax.axis_index("pf")
    here_index = lax.axis_index("ctx")
    page_rows, request_count, page_length, latent_width = latent_pages.shape
    row_count = page_rows * request_count
    capacity = max(2, 9 * row_count // (8 * context_devices))
    slot_count = context_devices * capacity
    score_scale = 1.0 / math.sqrt(HD_DIM)
    flat_pages = latent_pages.reshape(row_count, page_length, latent_width)
    lane_target = lax.dynamic_index_in_dim(
        page_target.reshape(context_devices, lane_count, row_count), lane_index, 1, keepdims=False
    )
    lane_filled = lax.dynamic_index_in_dim(
        page_count.reshape(context_devices, lane_count, row_count), lane_index, 1, keepdims=False
    )
    own_target = lax.dynamic_index_in_dim(lane_target, here_index, 0, keepdims=False)
    row_ids = jnp.arange(row_count, dtype=jnp.int32)
    targets = jnp.arange(context_devices, dtype=jnp.int32)
    chosen = (own_target[:, None] == targets[None, :]).astype(jnp.int32)
    row_rank = jnp.sum(jnp.cumsum(chosen, axis=0) * chosen, axis=1) - 1
    slot_of_row = own_target * capacity + row_rank
    source_row = jnp.full((slot_count,), row_count, jnp.int32).at[slot_of_row].set(row_ids)
    padded = jnp.concatenate(
        [flat_pages, jnp.zeros((1, page_length, latent_width), flat_pages.dtype)], axis=0
    )
    outgoing = jnp.take(padded, source_row, axis=0)
    stored = lax.all_to_all(outgoing, "ctx", split_axis=0, concat_axis=0, tiled=True)
    query_position = (context_length[None, :] + jnp.arange(STEPS, dtype=jnp.int32)[:, None]).astype(
        jnp.float32
    )
    heads_local = queries.shape[2] // HD_DIM
    turned = rotate(
        queries.astype(jnp.float32).reshape(STEPS, REQS, heads_local, HD_DIM),
        query_position[:, :, None],
    ).astype(jnp.bfloat16)
    gathered = lax.all_gather(
        turned.reshape(STEPS, REQS, heads_local * HD_DIM), "hd", axis=2, tiled=True
    )
    column_count = STEPS * REQS * GROUP
    query_columns = (
        gathered.reshape(STEPS, REQS, KVH, GROUP, HD_DIM)
        .transpose(2, 4, 0, 1, 3)
        .reshape(KVH, HD_DIM, column_count)
    )
    column_ids = jnp.arange(column_count, dtype=jnp.int32)
    column_step = column_ids // (REQS * GROUP)
    column_request = column_ids // GROUP % REQS
    request_match = column_request[:, None] == jnp.arange(REQS, dtype=jnp.int32)[None, :]
    column_limit = (
        jnp.sum(jnp.where(request_match, context_length[None, :], 0), axis=1) + column_step
    )
    incoming = (lane_target == here_index).astype(jnp.int32)
    arrive_rank = jnp.cumsum(incoming, axis=1) - 1
    arrive_slot = jnp.where(
        incoming > 0, targets[:, None] * capacity + arrive_rank, slot_count
    ).reshape(-1)
    sender_page = (
        (targets[:, None] * lane_count + lane_index) * page_rows + row_ids[None, :] // request_count
    ).reshape(-1)
    sender_request = jnp.broadcast_to(
        row_ids[None, :] % request_count, (context_devices, row_count)
    ).reshape(-1)
    page_of_slot = (
        jnp.zeros((slot_count + 1,), jnp.int32).at[arrive_slot].set(sender_page)[:slot_count]
    )
    request_of_slot = (
        jnp.zeros((slot_count + 1,), jnp.int32).at[arrive_slot].set(sender_request)[:slot_count]
    )
    count_of_slot = (
        jnp.zeros((slot_count + 1,), jnp.int32)
        .at[arrive_slot]
        .set(lane_filled.reshape(-1))[:slot_count]
    )
    page_total = stored.shape[0]
    block_count = page_total // page_total
    offsets = jnp.arange(PAGE, dtype=jnp.int32)
    token_position = page_of_slot[:, None] * PAGE + offsets[None, :]
    token_valid = offsets[None, :] < count_of_slot[:, None]
    token_request = jnp.broadcast_to(request_of_slot[:, None], (page_total, PAGE))
    grouped = (
        stored.reshape(block_count, page_total * PAGE, LATK + LATV),
        token_position.reshape(block_count, -1),
        token_valid.reshape(block_count, -1),
        token_request.reshape(block_count, -1),
    )

    def block_scores(rebuilt, position, valid_rows, request_rows):
        scores = (
            jnp.einsum("tkd,kdc->ktc", rebuilt, query_columns, preferred_element_type=jnp.float32)
            * score_scale
        )
        valid_mask = (
            valid_rows[:, None]
            & (request_rows[:, None] == column_request[None, :])
            & (position[:, None] <= column_limit[None, :])
        )
        return jnp.where(valid_mask[None], scores, -1e30)

    def rebuild(latent, position):
        rebuilt = jnp.dot(latent[:, :LATK], key_up, preferred_element_type=jnp.float32)
        return rotate(
            rebuilt.reshape(-1, KVH, HD_DIM), position.astype(jnp.float32)[:, None]
        ).astype(jnp.bfloat16)

    starting = (
        jnp.zeros((KVH, column_count, LATV), jnp.float32),
        jnp.zeros((KVH, column_count), jnp.float32),
    )

    def first_pass(pieces):
        latent, position, valid_rows, request_rows = pieces
        rebuilt = rebuild(latent, position)
        return (rebuilt, jnp.max(block_scores(rebuilt, position, valid_rows, request_rows), axis=1))

    rebuilt_all, peaks = lax.map(first_pass, grouped)
    global_peak = lax.pmax(jnp.max(peaks, axis=0), ("ctx", "hd", "pf"))

    def second_pass(carry, pieces):
        rebuilt, latent, position, valid_rows, request_rows = pieces
        weights = jnp.exp(
            block_scores(rebuilt, position, valid_rows, request_rows) - global_peak[:, None, :]
        )
        weight_total = carry[1] + jnp.sum(weights, axis=1)
        numerator = carry[0] + jnp.einsum(
            "ktc,tl->kcl",
            weights.astype(jnp.bfloat16),
            latent[:, LATK:],
            preferred_element_type=jnp.float32,
        )
        return ((numerator, weight_total), None)

    (numerator, weight_total), unused = lax.scan(second_pass, starting, (rebuilt_all,) + grouped)
    numerator, weight_total, running = (numerator, weight_total, global_peak)
    numerator, weight_total = (
        lax.psum_scatter(
            numerator.astype(jnp.bfloat16), "hd", scatter_dimension=0, tiled=True
        ).astype(jnp.float32),
        lax.psum_scatter(
            weight_total.astype(jnp.bfloat16), "hd", scatter_dimension=0, tiled=True
        ).astype(jnp.float32),
    )
    numerator, weight_total = (
        lax.psum(numerator.astype(jnp.bfloat16), ("ctx", "pf")).astype(jnp.float32),
        lax.psum(weight_total.astype(jnp.bfloat16), ("ctx", "pf")).astype(jnp.float32),
    )
    owned_heads = numerator.shape[0]
    context = (numerator / weight_total[..., None]).astype(jnp.bfloat16)
    value_heads = value_up.reshape(LATV, owned_heads, HD_DIM)
    result = jnp.einsum(
        "kcl,lkd->kcd", context, value_heads, preferred_element_type=jnp.float32
    ).astype(jnp.bfloat16)
    attended = (
        result.reshape(owned_heads, STEPS, REQS, GROUP, HD_DIM)
        .transpose(1, 2, 0, 3, 4)
        .reshape(STEPS, REQS, owned_heads * GROUP * HD_DIM)
    )
    return (attended, stored)


def solution(mesh):
    placed = (
        P(("ctx", "hd", "pf"), "grp", None, None),
        P(None, "grp", None),
        P(None, "grp"),
        P("grp"),
        P(None, "grp", "hd"),
        P(),
        P(None, "hd"),
    )
    return jax.shard_map(
        on_device,
        mesh=mesh,
        in_specs=placed,
        out_specs=(P(None, "grp", "hd"), P(("grp", "ctx", "hd", "pf"), None, None)),
        check_vma=False,
    )
```

profile of v0, /device:TPU:8, one launch (start us, length us, event | category | flops | bytes accessed | tf_op | source)
XLA Modules:
  0.0 227.3 jit_solution(9113171062007912551)
XLA Ops:
  7.2 0.9 copy.30
  8.3 0.2 reduce_window_sum.23
  8.7 1.0 scatter_custom_fusion.3
  9.7 1.8 concatenate.12
  11.5 2.4 %gather_fusion = bf16[144,16,512]{2,1,0:T(8,128)(2,1)} fusion(bf16[129,16,512]{2,1,0:T(8,128)(2,1)S(1)} %concatenate.12, s32[1024]{0:T(1024)S(1)} %pad_clamp_fusion), kind=kCustom, calls=%fused_computation | custom fusion | bytes 4719168 | tf_op jit(solution)/shard_map/jit(_take)/gather | solution.py:74
  13.9 3.4 %broadcast_select_fusion = bf16[144,16,512]{2,1,0:T(8,128)(2,1)} fusion(bf16[144,16,512]{2,1,0:T(8,128)(2,1)} %gather_fusion, pred[144]{0:T(512)(128)(4,1)S(1)} %compare_and_fusion.1), kind=kLoop, calls=%fused_computation.18 | loop fusion | flops 1179648 | bytes 4718736 | tf_op jit(solution)/shard_map/jit(_take)/select_n | solution.py:74
  17.3 5.3 %all-to-all-start = ((bf16[144,16,512]{2,1,0:T(8,128)(2,1)}), bf16[144,16,512]{2,1,0:T(8,128)(2,1)S(1)}, u32[]{:S(2)}, u32[]{:S(2)}) async-start(bf16[144,16,512]{2,1,0:T(8,128)(2,1)} %broadcast_select_fusion), calls=%async_computation | async-start | bytes 4718592 | tf_op jit(solution)/shard_map/all_to_all | solution.py:75
  22.6 0.3 reduce_window_sum.22
  23.1 2.4 %scatter_custom_fusion.2 = s32[145]{0:T(256)S(1)} fusion(s32[512]{0:T(512)S(1)} %bitcast.72, s32[512]{0:T(512)S(1)} %add_bitcast_fusion, s32[]{:T(128)} %constant.206.clone.1), kind=kCustom, calls=%fused_computation.81 | custom fusion | bytes 584 | tf_op jit(solution)/shard_map/scatter | solution.py:112
  25.9 2.4 %scatter_custom_fusion = s32[145]{0:T(256)S(1)} fusion(s32[512]{0:T(512)S(1)} %bitcast.73, s32[512]{0:T(512)S(1)} %bitcast.75, s32[]{:T(128)} %constant.206.clone.1), kind=kCustom, calls=%fused_computation.85 | custom fusion | bytes 584 | tf_op jit(solution)/shard_map/scatter | solution.py:120
  28.7 2.4 %scatter_custom_fusion.1 = s32[145]{0:T(256)S(1)} fusion(s32[512]{0:T(512)S(1)} %bitcast.74, s32[512]{0:T(512)S(1)} %broadcast_bitcast_fusion, s32[]{:T(128)} %constant.206.clone.1), kind=kCustom, calls=%fused_computation.83 | custom fusion | bytes 584 | tf_op jit(solution)/shard_map/scatter | solution.py:115
  31.7 5.8 %all_gather.3 = bf16[2,8,8192]{2,1,0:T(8,128)(2,1)S(1)} all-gather(bf16[2,8,4096]{2,1,0:T(8,128)(2,1)S(1)} %maximum_bitcast_fusion), channel_id=1, replica_groups=mesh['grp'=2,'ctx'=4,'hd'=2,'pf'=2] {'hd'}, dimensions={2}, use_global_device_ids=true | all-gather | bytes 393216 | tf_op jit(solution)/shard_map/all_gather | solution.py:84
  37.8 2.1 compare_and_fusion
  39.9 6.2 %multiply_cosine_fusion = (f32[2304,64]{1,0:T(8,128)}, f32[2304,64]{1,0:T(8,128)}) fusion(f32[64]{0:T(128)S(1)} %compare_select_fusion.6, f32[2304]{0:T(1024)S(1)} %convert_element_type.88), kind=kLoop, calls=%fused_computation.20 | loop fusion | flops 147456 | bytes 1189120 | tf_op jit(solution)/shard_map/while/body/eval_jaxpr/cos | solution.py:32
  46.1 27.0 %all-to-all-done = bf16[144,16,512]{2,1,0:T(8,128)(2,1)S(1)} async-done(((bf16[144,16,512]{2,1,0:T(8,128)(2,1)}), bf16[144,16,512]{2,1,0:T(8,128)(2,1)S(1)}, u32[]{:S(2)}, u32[]{:S(2)}) %all-to-all-start) | async-done | bytes 2359328 | tf_op jit(solution)/shard_map/all_to_all | solution.py:75
  73.1 1.4 fusion.13
  74.5 4.5 %fusion.34 = (f32[2304,8,64]{0,2,1:T(8,128)}, f32[2304,8,64]{0,2,1:T(8,128)}) fusion(f32[2304,8,128]{0,2,1:T(8,128)S(1)} %bitcast.61), kind=kLoop, calls=%fused_computation.91 | loop fusion | bytes 18874368 | tf_op jit(solution)/shard_map/while/body/eval_jaxpr/slice | solution.py:35
  79.1 7.6 %copy.41 = f32[2304,8,64]{2,0,1:T(8,128)} copy(f32[2304,8,64]{0,2,1:T(8,128)} %get-tuple-element.50) | data formatting | bytes 9437184
  86.6 7.5 %copy.42 = f32[2304,8,64]{2,0,1:T(8,128)} copy(f32[2304,8,64]{0,2,1:T(8,128)} %get-tuple-element.49) | data formatting | bytes 9437184
  94.2 8.1 %subtract_convert_fusion = (bf16[2304,8,64]{2,0,1:T(8,128)(2,1)S(1)}, bf16[2304,8,64]{2,0,1:T(8,128)(2,1)S(1)}) fusion(f32[2304,8,64]{2,0,1:T(8,128)} %copy.42, f32[2304,8,64]{2,0,1:T(8,128)} %copy.41, f32[2304,64]{1,0:T(8,128)} %get-tuple-element.54, f32[2304,64]{1,0:T(8,128)} %get-tuple-element.53), kind=kLoop, calls=%fused_computation.8 | loop fusion | flops 9437184 | bytes 15335424 | tf_op jit(solution)/shard_map/convert.4
  102.3 6.1 %fusion = (f32[8,128]{1,0:T(8,128)S(1)}, f32[8,2304,128]{2,1,0:T(8,128)}) fusion(pred[2304,128]{1,0:T(8,128)(4,1)S(1)} %compare_and_fusion, bf16[8,128,128]{1,2,0:T(8,128)(2,1)S(1)} %bitcast.65, bf16[2304,8,64]{2,0,1:T(8,128)(2,1)S(1)} %get-tuple-element.48, bf16[2304,8,64]{2,0,1:T(8,128)(2,1)S(1)} %get-tuple-element.47), kind=kOutput, calls=%fused_computation.9 | convolution fusion | flops 620493824 | bytes 14716928 | tf_op jit(solution)/shard_map/while/body/eval_jaxpr/tkd,kdc->ktc/dot_general | solution.py:137
  108.4 25.1 %pmax.7 = f32[8,128]{1,0:T(8,128)S(1)} all-reduce(f32[8,128]{1,0:T(8,128)S(1)} %get-tuple-element.69), channel_id=1, replica_groups=mesh['grp'=2,'ctx'=4,'hd'=2,'pf'=2] {'ctx','hd','pf'}, use_global_device_ids=true, to_apply=%region_9.10 | all-reduce | flops 1024 | bytes 8192 | tf_op jit(solution)/shard_map/pmax | solution.py:164
  133.5 7.4 %fusion.10 = bf16[8,128,256]{2,1,0:T(8,128)(2,1)} fusion(f32[8,2304,128]{2,1,0:T(8,128)} %get-tuple-element.70, f32[8,128]{1,0:T(8,128)S(1)} %pmax.7, pred[2304,128]{1,0:T(8,128)(4,1)S(1)} %compare_and_fusion, bf16[2304,512]{1,0:T(8,128)(2,1)S(1)} %bitcast.63), kind=kOutput, calls=%fused_computation.21 | convolution fusion | flops 1217658880 | bytes 11440128 | tf_op jit(solution)/shard_map/while/body/eval_jaxpr/ktc,tl->kcl/dot_general | solution.py:172
  141.0 0.6 dynamic-slice.3
  142.2 18.4 %reduce-scatter.2.cloned.1.call-done = bf16[4,128,256]{2,1,0:T(8,128)(2,1)} async-done(((bf16[8,128,256]{2,1,0:T(8,128)(2,1)}), bf16[4,128,256]{2,1,0:T(8,128)(2,1)}) %reduce-scatter.2.cloned.1.call-update) | async-done | bytes 262160 | tf_op jit(solution)/shard_map/reduce_scatter | solution.py:183
  160.7 5.7 %fusion.1 = bf16[8,128]{1,0:T(8,128)(2,1)S(1)} fusion(f32[8,2304,128]{2,1,0:T(8,128)} %get-tuple-element.70, f32[8,128]{1,0:T(8,128)S(1)} %pmax.7, pred[2304,128]{1,0:T(8,128)(4,1)S(1)} %compare_and_fusion), kind=kLoop, calls=%fused_computation.10 | loop fusion | flops 9436160 | bytes 9738240 | tf_op jit(solution)/shard_map/while/body/eval_jaxpr/reduce_sum | solution.py:171
  166.3 4.9 %all-reduce.1 = bf16[8,128]{1,0:T(8,128)(2,1)S(1)} all-reduce(bf16[8,128]{1,0:T(8,128)(2,1)S(1)} %fusion.1), channel_id=3, replica_groups=mesh['grp'=2,'ctx'=4,'hd'=2,'pf'=2] {'hd'}, use_global_device_ids=true, to_apply=%region_13.14.clone | all-reduce | flops 1024 | bytes 4096
  171.3 12.1 %psum.15 = bf16[4,128]{1,0:T(4,128)(2,1)S(1)} all-reduce(bf16[4,128]{1,0:T(4,128)(2,1)S(1)} %constant_dynamic-slice_fusion.2), channel_id=1, replica_groups=mesh['grp'=2,'ctx'=4,'hd'=2,'pf'=2] {'ctx','pf'}, use_global_device_ids=true, to_apply=%region_14.15 | all-reduce | flops 512 | bytes 2048 | tf_op jit(solution)/shard_map/psum | solution.py:192
  183.4 33.7 %all-reduce.4.cloned.1.call-done = bf16[4,128,256]{2,1,0:T(8,128)(2,1)} async-done(((bf16[4,128,256]{2,1,0:T(8,128)(2,1)}), bf16[4,128,256]{2,1,0:T(8,128)(2,1)}) %all-reduce.4.cloned.1.call-update) | async-done | bytes 262160 | tf_op jit(solution)/shard_map/psum | solution.py:191
  217.1 1.2 convolution_convert_fusion
  218.3 0.7 copy.38
  219.0 1.4 copy.53
  (59 shorter events, 2.1 us)
Async XLA Ops:
  7.2 66.0 %copy-start = (bf16[256,1024]{1,0:T(8,128)(2,1)S(1)}, bf16[256,1024]{1,0:T(8,128)(2,1)}, u32[]{:S(2)}) copy-start(bf16[256,1024]{1,0:T(8,128)(2,1)} %param.12) | copy-start | bytes 1572868
  13.8 11.8 %copy-start.3 = (s32[256,8]{0,1:T(8,128)S(1)}, s32[256,8]{0,1:T(8,128)}, u32[]{:S(2)}) copy-start(s32[256,8]{0,1:T(8,128)} %param.9) | copy-start | bytes 24580
  13.8 17.4 %copy-start.5 = (s32[8]{0:T(128)S(1)}, s32[8]{0:T(128)}, u32[]{:S(2)}) copy-start(s32[8]{0:T(128)} %param.10) | copy-start | bytes 100
  13.9 17.6 %copy-start.2 = (bf16[2,8,4096]{2,1,0:T(8,128)(2,1)S(1)}, bf16[2,8,4096]{2,1,0:T(8,128)(2,1)}, u32[]{:S(2)}) copy-start(bf16[2,8,4096]{2,1,0:T(8,128)(2,1)} %param.11) | copy-start | bytes 393220
  17.3 55.9 %all-to-all-start = ((bf16[144,16,512]{2,1,0:T(8,128)(2,1)}), bf16[144,16,512]{2,1,0:T(8,128)(2,1)S(1)}, u32[]{:S(2)}, u32[]{:S(2)}) async-start(bf16[144,16,512]{2,1,0:T(8,128)(2,1)} %broadcast_select_fusion), calls=%async_computation | async-start | bytes 4718592 | tf_op jit(solution)/shard_map/all_to_all | solution.py:75
  22.6 138.1 %reduce-scatter.2.cloned.1.call-start = ((), (), s32[]{:S(2)}) async-start(), calls=%async_computation.2 | async-start | bytes 786432 | tf_op jit(solution)/shard_map/reduce_scatter | solution.py:183
  133.5 7.5 %copy-start.6 = (u32[32]{0:T(128)S(1)}, u32[32]{0:T(128)}, u32[]{:S(2)}) copy-start(u32[32]{0:T(128)} %constant.244) | copy-start | bytes 388
  140.9 76.2 %all-reduce.4.cloned.1.call-start = ((), (), s32[]{:S(2)}) async-start(), calls=%async_computation.3 | async-start | bytes 524288 | tf_op jit(solution)/shard_map/psum | solution.py:191
  160.7 56.5 %copy-start.4 = (bf16[256,512]{1,0:T(8,128)(2,1)S(1)}, bf16[256,512]{1,0:T(8,128)(2,1)}, u32[]{:S(2)}) copy-start(bf16[256,512]{1,0:T(8,128)(2,1)} %param.13) | copy-start | bytes 786436
  160.7 59.8 %copy-start.1 = (bf16[256,1024]{1,0:T(8,128)(2,1)S(1)}, bf16[256,1024]{1,0:T(8,128)(2,1)}, u32[]{:S(2)}) copy-start(bf16[256,1024]{1,0:T(8,128)(2,1)} %param.12) | copy-start | bytes 1572868
Sparse Core Ops, SparseCore 0:
  141.1 19.5 reduce-scatter.1
  163.1 54.0 all-reduce.3
where the time goes:
time: 230 us; the launch traced here: 227 us
  waiting for transfers between devices  79.2 us (34%)
  blocking collectives  48 us (21%)
  local copies, waits for them, and re-layouts  36.5 us (16%)
  other arithmetic  27.1 us (12%)
  matrix products  16.2 us (7%)
  between operations  15 us (7%)
  starting transfers between devices  5.36 us (2%)
    psum x1, waiting for transfers between devices, on_device(): lax.psum(numerator.astype(jnp.bfloat16), ('ctx', 'pf')).astype(jnp.float32)  33.7 us
    all_to_all x1, waiting for transfers between devices, on_device(): lax.all_to_all(outgoing, 'ctx', split_axis=0, concat_axis=0, tiled=True)  27 us
    pmax x1, blocking collectives, on_device(): global_peak = lax.pmax(jnp.max(peaks, axis=0), ('ctx', 'hd', 'pf'))  25.1 us
    reduce_scatter x1, waiting for transfers between devices, on_device(): lax.psum_scatter(numerator.astype(jnp.bfloat16), 'hd', scatter_dimension=...  18.4 us
    unnamed x22, local copies, waits for them, and re-layouts  18.2 us
    psum x1, blocking collectives, on_device(): lax.psum(weight_total.astype(jnp.bfloat16), ('ctx', 'pf'))  12.1 us
    another operation x2, other arithmetic  8.26 us
    dot_general x1, matrix products, second_pass(): jnp.einsum('ktc,tl->kcl', weights.astype(jnp.bfloat16), latent[:, LATK:],...  7.38 us
  transfers between devices with their start and end apart: 3, of which 3 were waited for; matrix products, arithmetic and copies ran while one was open for 10% of the time, Pallas kernels for 0%

commit v1 on v0

v1 whole, which is shorter than its diff:
```python
import functools
import math

import jax
import jax.numpy as jnp
import numpy as np
from jax import lax
from jax.experimental import pallas as pl
from jax.experimental.pallas import tpu as pltpu
from jax.sharding import PartitionSpec as P

KVH = 8
GROUP = 8
HD_DIM = 128
LATK = 256
LATV = 256
PAGE = 16
STEPS = 2
REQS = 8
COLS = STEPS * GROUP
LANES = 128
MESH = pl.DeviceIdType.MESH
NEVER = -1e30


def frequencies(head_width):
    exponent = np.arange(0, head_width, 2).astype(np.float32) / np.float32(head_width)
    inverse = np.power(np.float32(500000.0), -exponent).astype(np.float32)
    wavelength = np.float32(2.0 * math.pi) / inverse
    smooth = (np.float32(8192.0) / wavelength - np.float32(1.0)) / np.float32(3.0)
    mixed = (1.0 - smooth) * inverse / 8.0 + smooth * inverse
    return np.where(
        wavelength > 8192.0, inverse / 8.0, np.where(wavelength < 2048.0, inverse, mixed)
    ).astype(np.float32)


def iota(shape, dim):
    return lax.broadcasted_iota(jnp.int32, shape, dim)


def kernel(
    n_ctx, n_hd, n_pf, capacity,
    pages, targets, counts, lengths, queries, key_up, value_up, freqs,
    stored, attended,
    packed, source_v, source_s, turned, q_all, part, stats, precv, pstats,
    summed, sstats, zrecv, zstats, result, table,
    page_send, page_recv, own_sem, source_sem, q_send, q_recv,
    part_send, part_recv, pst_send, pst_recv, z_send, z_recv, zst_send, zst_recv,
    out_send, out_recv,
):
    ctx, hd, pf = lax.axis_index("ctx"), lax.axis_index("hd"), lax.axis_index("pf")
    page_rows = pages.shape[0]
    rows = page_rows * REQS
    tokens = page_rows * PAGE
    device = (ctx * n_hd + hd) * n_pf + pf
    local_heads = KVH // n_hd
    per_req = local_heads * COLS
    own_reqs = REQS // n_pf

    def at(axis, index, offset, size):
        return {axis: lax.rem(index + offset, size)}

    plane_offsets = [(a, b) for a in range(n_hd) for b in range(n_pf) if a or b]
    out_offsets = [(a, b) for a in range(n_ctx) for b in range(n_pf) if a or b]

    barrier = pltpu.get_barrier_semaphore()
    greeted = 0
    for a, b in out_offsets:
        pl.semaphore_signal(
            barrier, inc=1, device_id_type=MESH,
            device_id={**at("ctx", ctx, a, n_ctx), **at("pf", pf, b, n_pf)},
        )
        greeted += 1
    for a, b in plane_offsets:
        if a:
            pl.semaphore_signal(
                barrier, inc=1, device_id_type=MESH,
                device_id={**at("hd", hd, a, n_hd), **at("pf", pf, b, n_pf)},
            )
            greeted += 1

    target_row = targets[pl.ds(device, 1), :]
    down, across = iota((rows, rows), 0), iota((rows, rows), 1)
    spread = jnp.broadcast_to(target_row, (rows, rows))
    target_col = jnp.sum(jnp.where(down == across, spread, 0), axis=1, keepdims=True)
    earlier = jnp.where((spread == target_col) & (across < down), 1, 0)
    slot_col = target_col * capacity + jnp.sum(earlier, axis=1, keepdims=True)
    width = source_v.shape[1]
    hit = slot_col == iota((rows, width), 1)
    source_v[...] = (
        jnp.sum(jnp.where(hit, iota((rows, width), 0) + 1, 0), axis=0, keepdims=True) - 1
    )
    to_scalars = pltpu.make_async_copy(source_v, source_s, source_sem)
    to_scalars.start()
    to_scalars.wait()

    def pack(block):
        def one(index, _):
            slot = block * capacity + index
            row = source_s[0, slot]
            safe = jnp.maximum(row, 0)
            page = pages[lax.div(safe, REQS), lax.rem(safe, REQS)]
            packed[slot] = jnp.where(row >= 0, page, jnp.zeros_like(page))
            return 0

        lax.fori_loop(0, capacity, one, 0)

    def page_copy(offset):
        block = lax.rem(ctx + offset, n_ctx)
        return pltpu.make_async_remote_copy(
            src_ref=packed.at[pl.ds(block * capacity, capacity)],
            dst_ref=stored.at[pl.ds(ctx * capacity, capacity)],
            send_sem=page_send.at[offset],
            recv_sem=page_recv.at[offset],
            device_id=at("ctx", ctx, offset, n_ctx),
            device_id_type=MESH,
        )

    half = n_ctx // 2
    order = sorted(range(1, n_ctx), key=lambda k: (abs(k - half), -k))
    page_copies = [page_copy(k) for k in order]
    for position, k in enumerate(order):
        pack(lax.rem(ctx + k, n_ctx))
        if position == 0:
            pl.semaphore_wait(barrier, greeted)
        page_copies[position].start()
    pack(ctx)
    own_copy = pltpu.make_async_copy(
        packed.at[pl.ds(ctx * capacity, capacity)],
        stored.at[pl.ds(ctx * capacity, capacity)],
        own_sem,
    )
    own_copy.start()

    lane = iota((REQS, HD_DIM), 1)
    sublane = iota((REQS, HD_DIM), 0)
    sign = jnp.where(lane < HD_DIM // 2, -1.0, 1.0).astype(jnp.float32)
    first_position = jnp.zeros((REQS, HD_DIM), jnp.int32)
    for r in range(REQS):
        first_position = jnp.where(sublane == r, lengths[r], first_position)
    frequency = jnp.broadcast_to(freqs[...], (REQS, HD_DIM))
    for s in range(STEPS):
        angle = (first_position + s).astype(jnp.float32) * frequency
        cosine, sine = jnp.cos(angle), jnp.sin(angle) * sign
        for head in range(local_heads * GROUP):
            k, g = head // GROUP, head % GROUP
            values = queries[s, :, head * HD_DIM:(head + 1) * HD_DIM].astype(jnp.float32)
            row = k * COLS + s * GROUP + g
            turned[row * REQS:(row + 1) * REQS, :] = (
                values * cosine + pltpu.roll(values, HD_DIM // 2, 1) * sine
            )
    for r in range(REQS):
        q_all[0, r] = turned[pl.ds(r, per_req, stride=REQS), :].astype(jnp.bfloat16)
    q_copies = []
    for a in range(1, n_hd):
        q_copies.append(
            pltpu.make_async_remote_copy(
                src_ref=q_all.at[0], dst_ref=q_all.at[a],
                send_sem=q_send.at[a], recv_sem=q_recv.at[a],
                device_id=at("hd", hd, a, n_hd), device_id_type=MESH,
            )
        )
        q_copies[-1].start()

    token = iota((tokens, HD_DIM), 0)
    angle = (device * tokens + token).astype(jnp.float32) * jnp.broadcast_to(
        freqs[...], (tokens, HD_DIM)
    )
    table[0] = jnp.cos(angle)
    table[1] = jnp.sin(angle) * jnp.where(iota((tokens, HD_DIM), 1) < HD_DIM // 2, -1.0, 1.0)

    own_counts = counts[pl.ds(pl.multiple_of(device * page_rows, page_rows), page_rows), :]
    pick = (iota((page_rows, tokens), 1) // PAGE == iota((page_rows, tokens), 0))
    spread_counts = lax.dot_general(
        own_counts.astype(jnp.float32).astype(jnp.bfloat16),
        jnp.where(pick, 1.0, 0.0).astype(jnp.bfloat16),
        (((0,), (0,)), ((), ())),
        preferred_element_type=jnp.float32,
    )
    column = iota((COLS, tokens), 1)
    step_of = iota((COLS, tokens), 0) // GROUP
    inside = (column % PAGE).astype(jnp.float32)
    position = device * tokens + column
    square = iota((LANES, LANES), 0) == iota((LANES, LANES), 1)
    request_of = iota((REQS, tokens), 0)

    for copy in q_copies:
        copy.wait()

    def attend(r, _):
        latent = pages[:, r].reshape(tokens, LATK + LATV)
        key_latent, value_latent = latent[:, :LATK], latent[:, LATK:]
        filled = jnp.sum(jnp.where(request_of == r, spread_counts, 0.0), axis=0, keepdims=True)
        valid = (inside < filled) & (position <= lengths[r] + step_of)
        peaks, totals = [], []
        for a in range(n_hd):
            owner = lax.rem(hd + n_hd - a, n_hd)
            for k in range(local_heads):
                start = pl.multiple_of((owner * local_heads + k) * HD_DIM, HD_DIM)
                rebuilt = jnp.dot(
                    key_latent, key_up[:, pl.ds(start, HD_DIM)],
                    preferred_element_type=jnp.float32,
                )
                keys = (
                    rebuilt * table[0] + pltpu.roll(rebuilt, HD_DIM // 2, 1) * table[1]
                ).astype(jnp.bfloat16)
                scores = lax.dot_general(
                    q_all[a, r, k * COLS:(k + 1) * COLS, :], keys,
                    (((1,), (1,)), ((), ())), preferred_element_type=jnp.float32,
                ) * (1.0 / math.sqrt(HD_DIM))
                masked = jnp.where(valid, scores, NEVER)
                peak = jnp.max(masked, axis=1, keepdims=True)
                weights = jnp.where(valid, jnp.exp(masked - peak), 0.0)
                peaks.append(peak)
                totals.append(jnp.sum(weights, axis=1, keepdims=True))
                part[a, r, k * COLS:(k + 1) * COLS, :] = jnp.dot(
                    weights.astype(jnp.bfloat16), value_latent,
                    preferred_element_type=jnp.float32,
                ).astype(jnp.bfloat16)
        for index, pieces in enumerate((peaks, totals)):
            tall = jnp.concatenate(pieces, axis=0)
            stats[index, pl.ds(r, 1), :] = jnp.sum(
                jnp.where(square, tall, 0.0), axis=0, keepdims=True
            )
        return 0

    lax.fori_loop(0, REQS, attend, 0)

    plane = []
    for a, b in plane_offsets:
        slot = a * n_pf + b
        there = {**at("hd", hd, a, n_hd), **at("pf", pf, b, n_pf)}
        other = lax.rem(pf + b, n_pf)
        mine = (n_hd - a) % n_hd
        plane.append(
            pltpu.make_async_remote_copy(
                src_ref=part.at[mine, pl.ds(other * own_reqs, own_reqs)],
                dst_ref=precv.at[slot],
                send_sem=part_send.at[slot], recv_sem=part_recv.at[slot],
                device_id=there, device_id_type=MESH,
            )
        )
        plane.append(
            pltpu.make_async_remote_copy(
                src_ref=stats, dst_ref=pstats.at[slot],
                send_sem=pst_send.at[slot], recv_sem=pst_recv.at[slot],
                device_id=there, device_id_type=MESH,
            )
        )
    for copy in plane:
        copy.start()
    for copy in plane:
        copy.wait()

    def to_column(row, shift):
        there = iota((per_req, LANES), 1) == iota((per_req, LANES), 0) + shift
        return jnp.sum(
            jnp.where(there, jnp.broadcast_to(row, (per_req, LANES)), 0.0),
            axis=1, keepdims=True,
        )

    sources = [(0, 0)] + plane_offsets
    for q in range(own_reqs):
        request = pf * own_reqs + q
        peaks, totals, numerators = [], [], []
        for a, b in sources:
            slot = a * n_pf + b
            shift = ((n_hd - a) % n_hd) * per_req
            if slot:
                rows_of = (pstats[slot, 0, pl.ds(request, 1), :], pstats[slot, 1, pl.ds(request, 1), :])
                numerators.append(precv[slot, q])
            else:
                rows_of = (stats[0, pl.ds(request, 1), :], stats[1, pl.ds(request, 1), :])
                numerators.append(part[0, request])
            peaks.append(to_column(rows_of[0], shift))
            totals.append(to_column(rows_of[1], shift))
        top = functools.reduce(jnp.maximum, peaks)
        total = jnp.zeros_like(top)
        numerator = jnp.zeros((per_req, LATV), jnp.float32)
        for peak, part_total, piece in zip(peaks, totals, numerators):
            factor = jnp.exp(peak - top)
            total = total + factor * part_total
            numerator = numerator + factor * piece.astype(jnp.float32)
        summed[q] = numerator.astype(jnp.bfloat16)
        corner = iota((per_req, LANES), 0) == iota((per_req, LANES), 1)
        for index, tall in enumerate((top, total)):
            sstats[index, q:q + 1, :] = jnp.sum(
                jnp.where(corner, tall, 0.0), axis=0, keepdims=True
            )

    def if_owner(index, body):
        if own_reqs >= n_ctx:
            body()
        else:
            pl.when(index < own_reqs)(body)

    def z_copies(offset):
        there = at("ctx", ctx, offset, n_ctx)
        other = lax.rem(ctx + offset, n_ctx)
        if own_reqs < n_ctx:
            other = jnp.minimum(other, own_reqs - 1)
        return (
            pltpu.make_async_remote_copy(
                src_ref=summed.at[other], dst_ref=zrecv.at[offset],
                send_sem=z_send.at[offset], recv_sem=z_recv.at[offset],
                device_id=there, device_id_type=MESH,
            ),
            pltpu.make_async_remote_copy(
                src_ref=sstats, dst_ref=zstats.at[offset],
                send_sem=zst_send.at[offset], recv_sem=zst_recv.at[offset],
                device_id=there, device_id_type=MESH,
            ),
        )

    def out_copy(a, b):
        slot = a * n_pf + b
        return pltpu.make_async_remote_copy(
            src_ref=result.at[pf, ctx], dst_ref=result.at[pf, ctx],
            send_sem=out_send.at[slot], recv_sem=out_recv.at[slot],
            device_id={**at("ctx", ctx, a, n_ctx), **at("pf", pf, b, n_pf)},
            device_id_type=MESH,
        )

    for offset in range(1, n_ctx):
        def start(offset=offset):
            for copy in z_copies(offset):
                copy.start()
        if_owner(lax.rem(ctx + offset, n_ctx), start)

    def finish():
        for offset in range(1, n_ctx):
            for copy in z_copies(offset):
                copy.wait_recv()
        peaks = [to_column(sstats[0, pl.ds(ctx, 1), :], 0)]
        totals = [to_column(sstats[1, pl.ds(ctx, 1), :], 0)]
        numerators = [summed[ctx]]
        for offset in range(1, n_ctx):
            peaks.append(to_column(zstats[offset, 0, pl.ds(ctx, 1), :], 0))
            totals.append(to_column(zstats[offset, 1, pl.ds(ctx, 1), :], 0))
            numerators.append(zrecv[offset])
        top = functools.reduce(jnp.maximum, peaks)
        total = jnp.zeros_like(top)
        numerator = jnp.zeros((per_req, LATV), jnp.float32)
        for peak, part_total, piece in zip(peaks, totals, numerators):
            factor = jnp.exp(peak - top)
            total = total + factor * part_total
            numerator = numerator + factor * piece.astype(jnp.float32)
        context = (numerator / total).astype(jnp.bfloat16)
        for k in range(local_heads):
            result[pf, ctx, k * COLS:(k + 1) * COLS, :] = jnp.dot(
                context[k * COLS:(k + 1) * COLS],
                value_up[:, k * HD_DIM:(k + 1) * HD_DIM],
                preferred_element_type=jnp.float32,
            ).astype(jnp.bfloat16)
        for a, b in out_offsets:
            out_copy(a, b).start()

    if_owner(ctx, finish)
    for offset in range(1, n_ctx):
        def sent(offset=offset):
            for copy in z_copies(offset):
                copy.wait_send()
        if_owner(lax.rem(ctx + offset, n_ctx), sent)
    for a, b in out_offsets:
        def arrived(a=a, b=b):
            out_copy(a, b).wait_recv()
        if_owner(lax.rem(ctx + n_ctx - a, n_ctx), arrived)

    def left():
        for a, b in out_offsets:
            out_copy(a, b).wait_send()

    if_owner(ctx, left)
    attended[...] = result[:, :own_reqs]
    own_copy.wait()
    for copy in page_copies:
        copy.wait()


def on_device(latent_pages, page_target, page_count, context_length, queries, key_up, value_up):
    n_ctx, n_hd, n_pf = lax.axis_size("ctx"), lax.axis_size("hd"), lax.axis_size("pf")
    page_rows, request_count, page_length, latent_width = latent_pages.shape
    row_count = page_rows * request_count
    capacity = max(2, 9 * row_count // (8 * n_ctx))
    slot_count = n_ctx * capacity
    local_heads = KVH // n_hd
    per_req = local_heads * COLS
    own_reqs = REQS // n_pf
    n_plane = n_hd * n_pf
    targets = page_target.reshape(-1, row_count)
    half = frequencies(HD_DIM)
    freqs = jnp.asarray(np.concatenate([half, half])[None, :])
    vmem = pl.BlockSpec(memory_space=pltpu.VMEM)
    dma = pltpu.SemaphoreType.DMA
    stored, rows = pl.pallas_call(
        functools.partial(kernel, n_ctx, n_hd, n_pf, capacity),
        out_shape=(
            jax.ShapeDtypeStruct((slot_count, page_length, latent_width), jnp.bfloat16),
            jax.ShapeDtypeStruct((n_pf, own_reqs, per_req, HD_DIM), jnp.bfloat16),
        ),
        in_specs=[
            vmem, vmem, vmem, pl.BlockSpec(memory_space=pltpu.SMEM), vmem, vmem, vmem, vmem,
        ],
        out_specs=(pl.BlockSpec(memory_space=pl.ANY), vmem),
        scratch_shapes=[
            pltpu.VMEM((slot_count, page_length, latent_width), jnp.bfloat16),
            pltpu.VMEM((1, -(-slot_count // LANES) * LANES), jnp.int32),
            pltpu.SMEM((1, -(-slot_count // LANES) * LANES), jnp.int32),
            pltpu.VMEM((per_req * REQS, HD_DIM), jnp.float32),
            pltpu.VMEM((n_hd, REQS, per_req, HD_DIM), jnp.bfloat16),
            pltpu.VMEM((n_hd, REQS, per_req, LATV), jnp.bfloat16),
            pltpu.VMEM((2, REQS, LANES), jnp.float32),
            pltpu.VMEM((n_plane, own_reqs, per_req, LATV), jnp.bfloat16),
            pltpu.VMEM((n_plane, 2, REQS, LANES), jnp.float32),
            pltpu.VMEM((own_reqs, per_req, LATV), jnp.bfloat16),
            pltpu.VMEM((2, own_reqs, LANES), jnp.float32),
            pltpu.VMEM((n_ctx, per_req, LATV), jnp.bfloat16),
            pltpu.VMEM((n_ctx, 2, own_reqs, LANES), jnp.float32),
            pltpu.VMEM((n_pf, n_ctx, per_req, HD_DIM), jnp.bfloat16),
            pltpu.VMEM((2, page_rows * PAGE, HD_DIM), jnp.float32),
            dma((n_ctx,)), dma((n_ctx,)), dma, dma, dma((n_hd,)), dma((n_hd,)),
            dma((n_plane,)), dma((n_plane,)), dma((n_plane,)), dma((n_plane,)),
            dma((n_ctx,)), dma((n_ctx,)), dma((n_ctx,)), dma((n_ctx,)),
            dma((n_ctx * n_pf,)), dma((n_ctx * n_pf,)),
        ],
        compiler_params=pltpu.CompilerParams(
            collective_id=0, has_side_effects=True, vmem_limit_bytes=40 * 1024 * 1024
        ),
    )(latent_pages, targets, page_count, context_length, queries, key_up, value_up, freqs)
    attended = (
        rows.reshape(REQS, local_heads, STEPS, GROUP, HD_DIM)
        .transpose(2, 0, 1, 3, 4)
        .reshape(STEPS, REQS, local_heads * GROUP * HD_DIM)
    )
    return (attended, stored)


def solution(mesh):
    placed = (
        P(("ctx", "hd", "pf"), "grp", None, None),
        P(None, "grp", None),
        P(None, "grp"),
        P("grp"),
        P(None, "grp", "hd"),
        P(),
        P(None, "hd"),
    )
    return jax.shard_map(
        on_device,
        mesh=mesh,
        in_specs=placed,
        out_specs=(P(None, "grp", "hd"), P(("grp", "ctx", "hd", "pf"), None, None)),
        check_vma=False,
    )
```

time: 230 us -> 76.7 us (0.33)
  the two profiles are of different devices: /device:TPU:8 before, /device:TPU:0 now
where the time goes in v1:
time: 76.7 us; the launch traced here: 76.3 us
  Pallas kernels  66 us (86%)
  local copies, waits for them, and re-layouts  9.69 us (13%)
    pallas_call x1, Pallas kernels, on_device(): pl.pallas_call(functools.partial(kernel, n_ctx, n_hd, n_pf, capacity), ou...  66 us
    unnamed x15, local copies, waits for them, and re-layouts  8.84 us

profile of v1, /device:TPU:0, one launch (start us, length us, event | category | flops | bytes accessed | tf_op | source)
XLA Modules:
  0.0 76.3 jit_solution(4825158279637670925)
XLA Ops:
  0.6 0.8 %copy.13 = s32[256,8,1]{1,0,2:T(8,128)S(1)} copy(s32[256,8,1]{0,2,1:T(1,128)} %param.9) | data formatting | bytes 16384 | tf_op args[1]
  1.5 0.1 reshape.13.targets
  1.6 0.8 %copy.14.counts = s32[256,8]{1,0:T(8,128)S(1)} copy(s32[256,8]{0,1:T(8,128)} %param.10) | data formatting | bytes 16384 | tf_op args[2]
  2.4 0.0 copy-start
  2.4 1.6 %copy-done = bf16[16,8,16,512]{3,2,1,0:T(8,128)(2,1)S(1)} copy-done((bf16[16,8,16,512]{3,2,1,0:T(8,128)(2,1)S(1)}, bf16[16,8,16,512]{3,2,1,0:T(8,128)(2,1)}, u32[]{:S(2)}) %copy-start) | copy-done | bytes 2097176
  4.0 0.0 copy-start.1
  4.0 1.0 %copy-done.1 = bf16[256,1024]{1,0:T(8,128)(2,1)S(1)} copy-done((bf16[256,1024]{1,0:T(8,128)(2,1)S(1)}, bf16[256,1024]{1,0:T(8,128)(2,1)}, u32[]{:S(2)}) %copy-start.1) | copy-done | bytes 524312
  5.0 0.0 copy-start.2
  5.0 0.9 %copy-done.2 = bf16[256,512]{1,0:T(8,128)(2,1)S(1)} copy-done((bf16[256,512]{1,0:T(8,128)(2,1)S(1)}, bf16[256,512]{1,0:T(8,128)(2,1)}, u32[]{:S(2)}) %copy-start.2) | copy-done | bytes 262168
  6.0 0.0 copy-start.3
  6.0 0.9 %copy-done.3 = bf16[2,8,4096]{2,1,0:T(8,128)(2,1)S(1)} copy-done((bf16[2,8,4096]{2,1,0:T(8,128)(2,1)S(1)}, bf16[2,8,4096]{2,1,0:T(8,128)(2,1)}, u32[]{:S(2)}) %copy-start.3) | copy-done | bytes 131096
  6.9 0.0 copy-start.4
  6.9 0.7 copy-done.4
  7.5 0.0 copy-start.5
  7.5 0.7 copy-done.5
  8.2 66.0 %shard_map.95 = (bf16[144,16,512]{2,1,0:T(8,128)(2,1)S(1)}, bf16[2,4,64,128]{3,2,1,0:T(8,128)(2,1)S(1)}) custom-call(bf16[16,8,16,512]{3,2,1,0:T(8,128)(2,1)S(1)} %copy-done, s32[16,128]{1,0:T(8,128)S(1)} %reshape.13.targets, s32[256,8]{1,0:T(8,128)S(1)} %copy.14.counts, s32[8]{0:T(128)S(1)} %copy-done.4, bf16[2,8,4096]{2,1,0:T(8,128)(2,1)S(1)} %copy-done.3, ...), custom_call_target="tpu_custom_call" | custom-call | tf_op jit(solution)/shard_map/pallas_call | solution.py:395
  74.2 0.7 copy.15
  74.9 1.4 %copy.17 = bf16[144,16,512]{2,1,0:T(8,128)(2,1)} copy(bf16[144,16,512]{2,1,0:T(8,128)(2,1)S(1)} %get-tuple-element.9) | data formatting | bytes 4718592
Async XLA Ops:
  2.4 1.6 %copy-start = (bf16[16,8,16,512]{3,2,1,0:T(8,128)(2,1)S(1)}, bf16[16,8,16,512]{3,2,1,0:T(8,128)(2,1)}, u32[]{:S(2)}) copy-start(bf16[16,8,16,512]{3,2,1,0:T(8,128)(2,1)} %pages.1) | copy-start | bytes 6291460
  4.0 1.0 %copy-start.1 = (bf16[256,1024]{1,0:T(8,128)(2,1)S(1)}, bf16[256,1024]{1,0:T(8,128)(2,1)}, u32[]{:S(2)}) copy-start(bf16[256,1024]{1,0:T(8,128)(2,1)} %key_up.1) | copy-start | bytes 1572868
  5.0 0.9 %copy-start.2 = (bf16[256,512]{1,0:T(8,128)(2,1)S(1)}, bf16[256,512]{1,0:T(8,128)(2,1)}, u32[]{:S(2)}) copy-start(bf16[256,512]{1,0:T(8,128)(2,1)} %value_up.1) | copy-start | bytes 786436
  6.0 0.9 %copy-start.3 = (bf16[2,8,4096]{2,1,0:T(8,128)(2,1)S(1)}, bf16[2,8,4096]{2,1,0:T(8,128)(2,1)}, u32[]{:S(2)}) copy-start(bf16[2,8,4096]{2,1,0:T(8,128)(2,1)} %queries.1) | copy-start | bytes 393220
  6.9 0.7 copy-start.4
  7.5 0.7 copy-start.5

commit v2 on v1

v2 whole, which is shorter than its diff:
```python
import functools
import math

import jax
import jax.numpy as jnp
import numpy as np
from jax import lax
from jax.experimental import pallas as pl
from jax.experimental.pallas import tpu as pltpu
from jax.sharding import PartitionSpec as P

KVH = 8
GROUP = 8
HD_DIM = 128
LATK = 256
LATV = 256
PAGE = 16
STEPS = 2
REQS = 8
COLS = STEPS * GROUP
LANES = 128
MESH = pl.DeviceIdType.MESH
NEVER = -1e30
EARLY, LATE, NEAR = 36, 6, 18


def frequencies(head_width):
    exponent = np.arange(0, head_width, 2).astype(np.float32) / np.float32(head_width)
    inverse = np.power(np.float32(500000.0), -exponent).astype(np.float32)
    wavelength = np.float32(2.0 * math.pi) / inverse
    smooth = (np.float32(8192.0) / wavelength - np.float32(1.0)) / np.float32(3.0)
    mixed = (1.0 - smooth) * inverse / 8.0 + smooth * inverse
    return np.where(
        wavelength > 8192.0, inverse / 8.0, np.where(wavelength < 2048.0, inverse, mixed)
    ).astype(np.float32)


def iota(shape, dim):
    return lax.broadcasted_iota(jnp.int32, shape, dim)


def kernel(
    n_ctx, n_hd, n_pf, capacity,
    pages_h, targets_h, counts_h, lengths_h, queries_h, key_up_h, value_up_h, freqs_h,
    stored, attended,
    pages, targets, counts, lengths, queries, key_up, value_up, freqs,
    packed, source_v, source_s, turned, q_all, part, stats, precv, pstats,
    summed, sstats, zrecv, zstats, result, table,
    in_sem, page_send, page_recv, own_sem, source_sem, q_send, q_recv,
    part_send, part_recv, pst_send, pst_recv, z_send, z_recv, zst_send, zst_recv,
    out_send, out_recv, fwd_send, fwd_recv,
):
    ctx, hd, pf = lax.axis_index("ctx"), lax.axis_index("hd"), lax.axis_index("pf")
    page_rows = pages.shape[0]
    rows = page_rows * REQS
    tokens = page_rows * PAGE
    device = (ctx * n_hd + hd) * n_pf + pf
    local_heads = KVH // n_hd
    per_req = local_heads * COLS
    own_reqs = REQS // n_pf
    plane_offsets = [(a, b) for a in range(n_hd) for b in range(n_pf) if a or b]

    def at(axis, index, offset, size):
        return {axis: lax.rem(index + offset, size)}

    barrier = pltpu.get_barrier_semaphore()
    for x in range(1, n_ctx):
        pl.semaphore_signal(barrier, inc=1, device_id_type=MESH, device_id={"ctx": ctx ^ x})
    for a, b in plane_offsets:
        pl.semaphore_signal(
            barrier, inc=1, device_id_type=MESH,
            device_id={**at("hd", hd, a, n_hd), **at("pf", pf, b, n_pf)},
        )
    greeted = n_ctx - 1 + len(plane_offsets)

    loads = [
        pltpu.make_async_copy(there, here, in_sem.at[index])
        for index, (there, here) in enumerate((
            (targets_h, targets), (pages_h, pages), (lengths_h, lengths), (freqs_h, freqs),
            (queries_h, queries), (counts_h, counts), (key_up_h, key_up),
            (value_up_h, value_up),
        ))
    ]
    for load in loads:
        load.start()
    loads[0].wait()

    total_pages = targets.shape[2]
    tall = jnp.concatenate([targets[r] for r in range(REQS)] * page_rows, axis=0)
    own_page = iota((rows, total_pages), 0) // REQS + device * page_rows
    target_col = jnp.sum(
        jnp.where(iota((rows, total_pages), 1) == own_page, tall, 0), axis=1, keepdims=True
    )
    down, across = iota((rows, rows), 0), iota((rows, rows), 1)
    target_row = jnp.sum(jnp.where(down == across, target_col, 0), axis=0, keepdims=True)
    earlier = jnp.where((target_row == target_col) & (across < down), 1, 0)
    slot_col = target_col * capacity + jnp.sum(earlier, axis=1, keepdims=True)
    width = source_v.shape[1]
    hit = slot_col == iota((rows, width), 1)
    source_v[...] = (
        jnp.sum(jnp.where(hit, iota((rows, width), 0) + 1, 0), axis=0, keepdims=True) - 1
    )
    to_scalars = pltpu.make_async_copy(source_v, source_s, source_sem)
    to_scalars.start()
    to_scalars.wait()
    loads[1].wait()

    def pack(block):
        def one(index, _):
            slot = block * capacity + index
            row = source_s[0, slot]
            safe = jnp.maximum(row, 0)
            page = pages[lax.div(safe, REQS), lax.rem(safe, REQS)]
            packed[slot] = jnp.where(row >= 0, page, jnp.zeros_like(page))
            return 0

        lax.fori_loop(0, capacity, one, 0)

    order = list(range(n_ctx // 2, n_ctx)) + list(range(1, n_ctx // 2))
    early, late, near = order[:n_ctx // 4], order[n_ctx // 4:n_ctx // 2], order[n_ctx // 2:]
    cuts = (EARLY * capacity // 36, LATE * capacity // 36, NEAR * capacity // 36)
    pieces = (
        [(x, 0, cuts[0]) for x in early] + [(x, 0, cuts[2]) for x in near],
        [(x, cuts[0], capacity) for x in early] + [(x, 0, cuts[1]) for x in late],
        [(x, cuts[1], capacity) for x in late] + [(x, cuts[2], capacity) for x in near],
    )
    page_copies = []

    def send_pages(stage):
        for x, low, high in pieces[stage]:
            if low == high:
                continue
            block = ctx ^ x
            slot = 2 * x + (1 if low else 0)
            copy = pltpu.make_async_remote_copy(
                src_ref=packed.at[pl.ds(block * capacity + low, high - low)],
                dst_ref=stored.at[pl.ds(ctx * capacity + low, high - low)],
                send_sem=page_send.at[slot],
                recv_sem=page_recv.at[slot],
                device_id={"ctx": block},
                device_id_type=MESH,
            )
            copy.start()
            page_copies.append(copy)

    for x in early + near:
        pack(ctx ^ x)
    pl.semaphore_wait(barrier, greeted)
    send_pages(0)
    for x in late:
        pack(ctx ^ x)
    pack(ctx)
    own_copy = pltpu.make_async_copy(
        packed.at[pl.ds(ctx * capacity, capacity)],
        stored.at[pl.ds(ctx * capacity, capacity)],
        own_sem,
    )
    own_copy.start()

    for load in loads[2:]:
        load.wait()
    lane = iota((REQS, HD_DIM), 1)
    sublane = iota((REQS, HD_DIM), 0)
    sign = jnp.where(lane < HD_DIM // 2, -1.0, 1.0).astype(jnp.float32)
    first_position = jnp.zeros((REQS, HD_DIM), jnp.int32)
    for r in range(REQS):
        first_position = jnp.where(sublane == r, lengths[r], first_position)
    frequency = jnp.broadcast_to(freqs[...], (REQS, HD_DIM))
    for s in range(STEPS):
        angle = (first_position + s).astype(jnp.float32) * frequency
        cosine, sine = jnp.cos(angle), jnp.sin(angle) * sign
        for head in range(local_heads * GROUP):
            k, g = head // GROUP, head % GROUP
            values = queries[s, :, head * HD_DIM:(head + 1) * HD_DIM].astype(jnp.float32)
            row = k * COLS + s * GROUP + g
            turned[row * REQS:(row + 1) * REQS, :] = (
                values * cosine + pltpu.roll(values, HD_DIM // 2, 1) * sine
            )
    for r in range(REQS):
        q_all[0, r] = turned[pl.ds(r, per_req, stride=REQS), :].astype(jnp.bfloat16)
    q_copies = []
    for a in range(1, n_hd):
        q_copies.append(
            pltpu.make_async_remote_copy(
                src_ref=q_all.at[0], dst_ref=q_all.at[a],
                send_sem=q_send.at[a], recv_sem=q_recv.at[a],
                device_id=at("hd", hd, a, n_hd), device_id_type=MESH,
            )
        )
        q_copies[-1].start()

    token = iota((tokens, HD_DIM), 0)
    angle = (device * tokens + token).astype(jnp.float32) * jnp.broadcast_to(
        freqs[...], (tokens, HD_DIM)
    )
    table[0] = jnp.cos(angle)
    table[1] = jnp.sin(angle) * jnp.where(iota((tokens, HD_DIM), 1) < HD_DIM // 2, -1.0, 1.0)

    pick = iota((total_pages, tokens), 0) == iota((total_pages, tokens), 1) // PAGE + device * page_rows
    spread_counts = jnp.dot(
        counts[...].astype(jnp.float32).astype(jnp.bfloat16),
        jnp.where(pick, 1.0, 0.0).astype(jnp.bfloat16),
        preferred_element_type=jnp.float32,
    )
    all_cols = KVH * COLS
    column = iota((all_cols, tokens), 1)
    step_of = iota((all_cols, tokens), 0) // GROUP % STEPS
    inside = (iota((1, tokens), 1) % PAGE).astype(jnp.float32)
    reach = device * tokens + column - step_of
    square = iota((LANES, LANES), 0) == iota((LANES, LANES), 1)
    request_of = iota((REQS, tokens), 0)

    for copy in q_copies:
        copy.wait()

    def part_copy(a, b, q):
        slot = a * n_pf + b
        other = lax.rem(pf + b, n_pf)
        return pltpu.make_async_remote_copy(
            src_ref=part.at[(n_hd - a) % n_hd, other * own_reqs + q],
            dst_ref=precv.at[slot, q],
            send_sem=part_send.at[slot, q], recv_sem=part_recv.at[slot, q],
            device_id={**at("hd", hd, a, n_hd), **at("pf", pf, b, n_pf)},
            device_id_type=MESH,
        )

    def attend(b, q):
        r = lax.rem(pf + b, n_pf) * own_reqs + q
        latent = pages[:, r].reshape(tokens, LATK + LATV)
        key_latent, value_latent = latent[:, :LATK], latent[:, LATK:]
        filled = jnp.sum(jnp.where(request_of == r, spread_counts, 0.0), axis=0, keepdims=True)
        valid = (inside < filled) & (reach <= lengths[r])
        scores = []
        for a in range(n_hd):
            owner = lax.rem(hd + n_hd - a, n_hd)
            start = pl.multiple_of(owner * local_heads * HD_DIM, HD_DIM)
            rebuilt = jnp.dot(
                key_latent, key_up[:, pl.ds(start, local_heads * HD_DIM)],
                preferred_element_type=jnp.float32,
            )
            for k in range(local_heads):
                plain = rebuilt[:, k * HD_DIM:(k + 1) * HD_DIM]
                keys = (
                    plain * table[0] + pltpu.roll(plain, HD_DIM // 2, 1) * table[1]
                ).astype(jnp.bfloat16)
                scores.append(lax.dot_general(
                    q_all[a, r, k * COLS:(k + 1) * COLS, :], keys,
                    (((1,), (1,)), ((), ())), preferred_element_type=jnp.float32,
                ))
        scores = jnp.concatenate(scores, axis=0) * (1.0 / math.sqrt(HD_DIM))
        masked = jnp.where(valid, scores, NEVER)
        peak = jnp.max(masked, axis=1, keepdims=True)
        weights = jnp.where(valid, jnp.exp(masked - peak), 0.0)
        total = jnp.sum(weights, axis=1, keepdims=True)
        numerator = jnp.dot(
            weights.astype(jnp.bfloat16), value_latent, preferred_element_type=jnp.float32
        ).astype(jnp.bfloat16)
        for a in range(n_hd):
            part[a, r] = numerator[a * per_req:(a + 1) * per_req]
            if a or b:
                part_copy((n_hd - a) % n_hd, b, q).start()
        for index, tall in enumerate((peak, total)):
            stats[index, pl.ds(r, 1), :] = jnp.sum(
                jnp.where(square, tall, 0.0), axis=0, keepdims=True
            )

    for b in list(range(1, n_pf)) + [0]:
        def one_request(q, _, b=b):
            attend(b, q)
            return 0

        lax.fori_loop(0, own_reqs, one_request, 0)

    plane = [
        pltpu.make_async_remote_copy(
            src_ref=stats, dst_ref=pstats.at[a * n_pf + b],
            send_sem=pst_send.at[a * n_pf + b], recv_sem=pst_recv.at[a * n_pf + b],
            device_id={**at("hd", hd, a, n_hd), **at("pf", pf, b, n_pf)},
            device_id_type=MESH,
        )
        for a, b in plane_offsets
    ]
    for copy in plane:
        copy.start()
    for copy in plane:
        copy.wait()

    def to_column(row, shift):
        there = iota((per_req, LANES), 1) == iota((per_req, LANES), 0) + shift
        return jnp.sum(
            jnp.where(there, jnp.broadcast_to(row, (per_req, LANES)), 0.0),
            axis=1, keepdims=True,
        )

    def merge(peaks, totals, numerators):
        top = functools.reduce(jnp.maximum, peaks)
        total = jnp.zeros_like(top)
        numerator = jnp.zeros(numerators[0].shape, jnp.float32)
        for peak, part_total, piece in zip(peaks, totals, numerators):
            factor = jnp.exp(peak - top)
            total = total + factor * part_total
            numerator = numerator + factor * piece.astype(jnp.float32)
        return top, total, numerator

    for q in range(own_reqs):
        request = pf * own_reqs + q
        for a, b in plane_offsets:
            part_copy(a, b, q).wait()
        peaks, totals, numerators = [], [], []
        for a, b in [(0, 0)] + plane_offsets:
            slot = a * n_pf + b
            shift = ((n_hd - a) % n_hd) * per_req
            if slot:
                pair = (pstats[slot, 0, pl.ds(request, 1), :], pstats[slot, 1, pl.ds(request, 1), :])
                numerators.append(precv[slot, q])
            else:
                pair = (stats[0, pl.ds(request, 1), :], stats[1, pl.ds(request, 1), :])
                numerators.append(part[0, request])
            peaks.append(to_column(pair[0], shift))
            totals.append(to_column(pair[1], shift))
        top, total, numerator = merge(peaks, totals, numerators)
        numerator = numerator.astype(jnp.bfloat16)
        for k in range(local_heads):
            summed[q, k * COLS:(k + 1) * COLS, :] = jnp.dot(
                numerator[k * COLS:(k + 1) * COLS],
                value_up[:, k * HD_DIM:(k + 1) * HD_DIM],
                preferred_element_type=jnp.float32,
            ).astype(jnp.bfloat16)
        corner = iota((per_req, LANES), 0) == iota((per_req, LANES), 1)
        for index, tall in enumerate((top, total)):
            sstats[index, q:q + 1, :] = jnp.sum(
                jnp.where(corner, tall, 0.0), axis=0, keepdims=True
            )

    def if_owner(index, body):
        if own_reqs >= n_ctx:
            body()
        else:
            pl.when(index < own_reqs)(body)

    def z_copies(x):
        other = ctx ^ x
        mine = other if own_reqs >= n_ctx else jnp.minimum(other, own_reqs - 1)
        return (
            pltpu.make_async_remote_copy(
                src_ref=summed.at[mine], dst_ref=zrecv.at[x],
                send_sem=z_send.at[x], recv_sem=z_recv.at[x],
                device_id={"ctx": other}, device_id_type=MESH,
            ),
            pltpu.make_async_remote_copy(
                src_ref=sstats, dst_ref=zstats.at[x],
                send_sem=zst_send.at[x], recv_sem=zst_recv.at[x],
                device_id={"ctx": other}, device_id_type=MESH,
            ),
        )

    def out_copy(x, came):
        owner = ctx ^ x if came else ctx
        return pltpu.make_async_remote_copy(
            src_ref=result.at[pf, owner], dst_ref=result.at[pf, owner],
            send_sem=out_send.at[x], recv_sem=out_recv.at[x],
            device_id={"ctx": ctx ^ x}, device_id_type=MESH,
        )

    def forward(x, b, came):
        place = lax.rem(pf + n_pf - b, n_pf) if came else pf
        slot = (b - 1) * n_ctx + x
        return pltpu.make_async_remote_copy(
            src_ref=result.at[place, ctx ^ x], dst_ref=result.at[place, ctx ^ x],
            send_sem=fwd_send.at[slot], recv_sem=fwd_recv.at[slot],
            device_id=at("pf", pf, b, n_pf), device_id_type=MESH,
        )

    for x in order:
        def start(x=x):
            for copy in z_copies(x):
                copy.start()
        if_owner(ctx ^ x, start)
    send_pages(1)

    def finish():
        for x in range(1, n_ctx):
            for copy in z_copies(x):
                copy.wait_recv()
        peaks = [to_column(sstats[0, pl.ds(ctx, 1), :], 0)]
        totals = [to_column(sstats[1, pl.ds(ctx, 1), :], 0)]
        numerators = [summed[ctx]]
        for x in range(1, n_ctx):
            peaks.append(to_column(zstats[x, 0, pl.ds(ctx, 1), :], 0))
            totals.append(to_column(zstats[x, 1, pl.ds(ctx, 1), :], 0))
            numerators.append(zrecv[x])
        top, total, numerator = merge(peaks, totals, numerators)
        result[pf, ctx] = (numerator / total).astype(jnp.bfloat16)
        for x in order:
            out_copy(x, False).start()
        for b in range(1, n_pf):
            forward(0, b, False).start()

    if_owner(ctx, finish)
    send_pages(2)
    for x in range(1, n_ctx):
        def passed_on(x=x):
            out_copy(x, True).wait_recv()
            for b in range(1, n_pf):
                forward(x, b, False).start()
        if_owner(ctx ^ x, passed_on)
    for x in range(n_ctx):
        def arrived(x=x):
            for b in range(1, n_pf):
                forward(x, b, True).wait_recv()
                forward(x, b, False).wait_send()
            if x:
                for copy in z_copies(x):
                    copy.wait_send()
        if_owner(ctx ^ x, arrived)

    def left():
        for x in range(1, n_ctx):
            out_copy(x, False).wait_send()

    if_owner(ctx, left)
    attended[...] = result[:, :own_reqs]
    own_copy.wait()
    for copy in page_copies:
        copy.wait()


def on_device(latent_pages, page_target, page_count, context_length, queries, key_up, value_up):
    n_ctx, n_hd, n_pf = lax.axis_size("ctx"), lax.axis_size("hd"), lax.axis_size("pf")
    page_rows, request_count, page_length, latent_width = latent_pages.shape
    row_count = page_rows * request_count
    capacity = max(2, 9 * row_count // (8 * n_ctx))
    slot_count = n_ctx * capacity
    slot_lanes = -(-slot_count // LANES) * LANES
    local_heads = KVH // n_hd
    per_req = local_heads * COLS
    own_reqs = REQS // n_pf
    n_plane = n_hd * n_pf
    half = frequencies(HD_DIM)
    operands = (
        latent_pages, page_target.transpose(1, 2, 0), page_count.T, context_length,
        queries, key_up, value_up, jnp.asarray(np.concatenate([half, half])[None, :]),
    )
    hbm = pl.BlockSpec(memory_space=pltpu.HBM)
    bf16, f32 = jnp.bfloat16, jnp.float32
    vmem, dma = pltpu.VMEM, pltpu.SemaphoreType.DMA
    stored, rows = pl.pallas_call(
        functools.partial(kernel, n_ctx, n_hd, n_pf, capacity),
        out_shape=(
            jax.ShapeDtypeStruct((slot_count, page_length, latent_width), bf16),
            jax.ShapeDtypeStruct((n_pf, own_reqs, per_req, HD_DIM), bf16),
        ),
        in_specs=[hbm] * len(operands),
        out_specs=(pl.BlockSpec(memory_space=pl.ANY), pl.BlockSpec(memory_space=pltpu.VMEM)),
        scratch_shapes=[
            (pltpu.SMEM if index == 3 else vmem)(operand.shape, operand.dtype)
            for index, operand in enumerate(operands)
        ] + [
            vmem((slot_count, page_length, latent_width), bf16),
            vmem((1, slot_lanes), jnp.int32),
            pltpu.SMEM((1, slot_lanes), jnp.int32),
            vmem((per_req * REQS, HD_DIM), f32),
            vmem((n_hd, REQS, per_req, HD_DIM), bf16),
            vmem((n_hd, REQS, per_req, LATV), bf16),
            vmem((2, REQS, LANES), f32),
            vmem((n_plane, own_reqs, per_req, LATV), bf16),
            vmem((n_plane, 2, REQS, LANES), f32),
            vmem((own_reqs, per_req, HD_DIM), bf16),
            vmem((2, own_reqs, LANES), f32),
            vmem((n_ctx, per_req, HD_DIM), bf16),
            vmem((n_ctx, 2, own_reqs, LANES), f32),
            vmem((n_pf, n_ctx, per_req, HD_DIM), bf16),
            vmem((2, page_rows * PAGE, HD_DIM), f32),
            dma((len(operands),)),
            dma((2 * n_ctx,)), dma((2 * n_ctx,)), dma, dma, dma((n_hd,)), dma((n_hd,)),
            dma((n_plane, own_reqs)), dma((n_plane, own_reqs)), dma((n_plane,)), dma((n_plane,)),
            dma((n_ctx,)), dma((n_ctx,)), dma((n_ctx,)), dma((n_ctx,)),
            dma((n_ctx,)), dma((n_ctx,)), dma((n_ctx * n_pf,)), dma((n_ctx * n_pf,)),
        ],
        compiler_params=pltpu.CompilerParams(
            collective_id=0, has_side_effects=True, vmem_limit_bytes=58 * 1024 * 1024
        ),
    )(*operands)
    attended = (
        rows.reshape(REQS, local_heads, STEPS, GROUP, HD_DIM)
        .transpose(2, 0, 1, 3, 4)
        .reshape(STEPS, REQS, local_heads * GROUP * HD_DIM)
    )
    return (attended, stored)


def solution(mesh):
    placed = (
        P(("ctx", "hd", "pf"), "grp", None, None),
        P(None, "grp", None),
        P(None, "grp"),
        P("grp"),
        P(None, "grp", "hd"),
        P(),
        P(None, "hd"),
    )
    return jax.shard_map(
        on_device,
        mesh=mesh,
        in_specs=placed,
        out_specs=(P(None, "grp", "hd"), P(("grp", "ctx", "hd", "pf"), None, None)),
        check_vma=False,
    )
```

time: 76.7 us -> 66.2 us (0.86)
  the two profiles are of different devices: /device:TPU:0 before, /device:TPU:8 now
where the time goes in v2:
time: 66.2 us; the launch traced here: 66 us
  Pallas kernels  60.4 us (91%)
  local copies, waits for them, and re-layouts  4.92 us (7%)
    pallas_call x1, Pallas kernels, on_device(): pl.pallas_call(functools.partial(kernel, n_ctx, n_hd, n_pf, capacity), ou...  60.4 us
    unnamed x1, local copies, waits for them, and re-layouts  3.27 us
    transpose x1, local copies, waits for them, and re-layouts, on_device(): attended = rows.reshape(REQS, local_heads, STEPS, GROUP, HD_DIM).transpos...  1.65 us

profile of v2, /device:TPU:8, one launch (start us, length us, event | category | flops | bytes accessed | tf_op | source)
XLA Modules:
  0.0 66.0 jit_solution(13939499662504855672)
XLA Ops:
  0.6 60.4 %shard_map.95 = (bf16[144,16,512]{2,1,0:T(8,128)(2,1)}, bf16[2,4,64,128]{3,2,1,0:T(8,128)(2,1)}) custom-call(bf16[16,8,16,512]{3,2,1,0:T(8,128)(2,1)} %pages_h.1, s32[8,1,256]{2,1,0:T(1,128)} %bitcast.8, s32[8,256]{1,0:T(8,128)} %bitcast.9, s32[8]{0:T(128)} %lengths_h.1, bf16[2,8,4096]{2,1,0:T(8,128)(2,1)} %queries_h.1, bf16[256,1024]{1,0:T(8,128)(2,1)} %key_up_h.1, ...), custom_call_target="tpu_custom_call" | custom-call | tf_op jit(solution)/shard_map/pallas_call | solution.py:447
  61.1 1.6 %copy.10 = bf16[2,8,4,8,128]{4,1,3,2,0:T(8,128)(2,1)} copy(bf16[2,8,4,8,128]{4,3,0,2,1:T(8,128)(2,1)} %bitcast.7) | data formatting | bytes 262144 | tf_op jit(solution)/shard_map/transpose | solution.py:486
  62.7 3.3 %copy.12 = bf16[144,16,512]{2,1,0:T(8,128)(2,1)} copy(bf16[144,16,512]{2,1,0:T(8,128)(2,1)} %get-tuple-element.9) | data formatting | bytes 4718592

commit v3 on v2

--- a/solution.py
+++ b/solution.py
@@ -21,6 +21,7 @@
 LANES = 128
 MESH = pl.DeviceIdType.MESH
 NEVER = -1e30
+SPLITS = 8
 EARLY, LATE, NEAR = 36, 6, 18
 
 
@@ -114,7 +115,7 @@
             packed[slot] = jnp.where(row >= 0, page, jnp.zeros_like(page))
             return 0
 
-        lax.fori_loop(0, capacity, one, 0)
+        lax.fori_loop(0, capacity, one, 0, unroll=9)
 
     order = list(range(n_ctx // 2, n_ctx)) + list(range(1, n_ctx // 2))
     early, late, near = order[:n_ctx // 4], order[n_ctx // 4:n_ctx // 2], order[n_ctx // 2:]
@@ -422,6 +423,40 @@
     attended[...] = result[:, :own_reqs]
     own_copy.wait()
     for copy in page_copies:
+        copy.wait()
+
+
+def deliver(local_heads, stored_in, rows_in, stored, attended, rows, turned, pages, in_sem, out_sem, rows_sem):
+    load = pltpu.make_async_copy(rows_in, rows, rows_sem)
+    load.start()
+    count = in_sem.shape[0]
+    size = pages.shape[0] // count
+    spans = [pl.ds(part * size, size) for part in range(count)]
+    reads = [
+        pltpu.make_async_copy(stored_in.at[span], pages.at[span], in_sem.at[part])
+        for part, span in enumerate(spans)
+    ]
+    writes = [
+        pltpu.make_async_copy(pages.at[span], stored.at[span], out_sem.at[part])
+        for part, span in enumerate(spans)
+    ]
+    for copy in reads:
+        copy.start()
+    for read, write in zip(reads, writes):
+        read.wait()
+        write.start()
+    load.wait()
+    per_req = local_heads * COLS
+    turned[...] = rows[...].reshape(turned.shape).astype(jnp.float32)
+    for s in range(STEPS):
+        for k in range(local_heads):
+            for g in range(GROUP):
+                row = k * COLS + s * GROUP + g
+                column = (k * GROUP + g) * HD_DIM
+                attended[s, :, column:column + HD_DIM] = turned[
+                    pl.ds(row, REQS, stride=per_req), :
+                ].astype(jnp.bfloat16)
+    for copy in writes:
         copy.wait()
 
 
@@ -481,11 +516,24 @@
             collective_id=0, has_side_effects=True, vmem_limit_bytes=58 * 1024 * 1024
         ),
     )(*operands)
-    attended = (
-        rows.reshape(REQS, local_heads, STEPS, GROUP, HD_DIM)
-        .transpose(2, 0, 1, 3, 4)
-        .reshape(STEPS, REQS, local_heads * GROUP * HD_DIM)
-    )
+    stored, attended = pl.pallas_call(
+        functools.partial(deliver, local_heads),
+        out_shape=(
+            jax.ShapeDtypeStruct(stored.shape, bf16),
+            jax.ShapeDtypeStruct(queries.shape, bf16),
+        ),
+        in_specs=[hbm, hbm],
+        out_specs=(hbm, pl.BlockSpec(memory_space=pltpu.VMEM)),
+        scratch_shapes=[
+            vmem(rows.shape, bf16),
+            vmem((REQS * per_req, HD_DIM), f32),
+            vmem(stored.shape, bf16),
+            dma((SPLITS,)),
+            dma((SPLITS,)),
+            dma,
+        ],
+        compiler_params=pltpu.CompilerParams(vmem_limit_bytes=58 * 1024 * 1024),
+    )(stored, rows)
     return (attended, stored)
 
 

time: 66.2 us -> 63.9 us (0.965)
  local copies, waits for them, and re-layouts: 4.92 us -> 0 us
  Pallas kernels: 60.4 us -> 63 us
    unnamed x1 -> x0, local copies, waits for them, and re-layouts: 3.27 us -> none
    pallas_call x0 -> x1, Pallas kernels: none -> 3.16 us  [on_device(): pl.pallas_call(functools.partial(deliver, local_heads), out_shape=(jax.Sh...]
    transpose x1 -> x0, local copies, waits for them, and re-layouts: 1.65 us -> none  [on_device(): attended = rows.reshape(REQS, local_heads, STEPS, GROUP, HD_DIM).transpos...]
where the time goes in v3:
time: 63.9 us; the launch traced here: 63.7 us
  Pallas kernels  63 us (99%)
  between operations  0.64 us (1%)
    pallas_call x1, Pallas kernels, on_device(): pl.pallas_call(functools.partial(kernel, n_ctx, n_hd, n_pf, capacity), ou...  59.9 us
    pallas_call x1, Pallas kernels, on_device(): pl.pallas_call(functools.partial(deliver, local_heads), out_shape=(jax.Sh...  3.16 us

profile of v3, /device:TPU:8, one launch (start us, length us, event | category | flops | bytes accessed | tf_op | source)
XLA Modules:
  0.0 63.7 jit_solution(11172506457094261677)
XLA Ops:
  0.6 59.9 %shard_map.95 = (bf16[144,16,512]{2,1,0:T(8,128)(2,1)}, bf16[2,4,64,128]{3,2,1,0:T(8,128)(2,1)}) custom-call(bf16[16,8,16,512]{3,2,1,0:T(8,128)(2,1)} %pages_h.1, s32[8,1,256]{2,1,0:T(1,128)} %bitcast.2, s32[8,256]{1,0:T(8,128)} %bitcast.3, s32[8]{0:T(128)} %lengths_h.1, bf16[2,8,4096]{2,1,0:T(8,128)(2,1)} %queries_h.1, bf16[256,1024]{1,0:T(8,128)(2,1)} %key_up_h.1, ...), custom_call_target="tpu_custom_call" | custom-call | tf_op jit(solution)/shard_map/pallas_call | solution.py:482
  60.5 3.2 %shard_map.96 = (bf16[144,16,512]{2,1,0:T(8,128)(2,1)}, bf16[2,8,4096]{2,1,0:T(8,128)(2,1)}) custom-call(bf16[144,16,512]{2,1,0:T(8,128)(2,1)} %get-tuple-element.6.stored_in, bf16[2,4,64,128]{3,2,1,0:T(8,128)(2,1)} %get-tuple-element.7.rows_in), custom_call_target="tpu_custom_call" | custom-call | tf_op jit(solution)/shard_map/pallas_call | solution.py:519

commit v4 on v3

--- a/solution.py
+++ b/solution.py
@@ -22,7 +22,7 @@
 MESH = pl.DeviceIdType.MESH
 NEVER = -1e30
 SPLITS = 8
-EARLY, LATE, NEAR = 36, 6, 18
+EARLY, LATE, NEAR = 36, 9, 36
 
 
 def frequencies(head_width):
@@ -121,7 +121,8 @@
     early, late, near = order[:n_ctx // 4], order[n_ctx // 4:n_ctx // 2], order[n_ctx // 2:]
     cuts = (EARLY * capacity // 36, LATE * capacity // 36, NEAR * capacity // 36)
     pieces = (
-        [(x, 0, cuts[0]) for x in early] + [(x, 0, cuts[2]) for x in near],
+        [(x, 0, cuts[0]) for x in early],
+        [(x, 0, cuts[2]) for x in near],
         [(x, cuts[0], capacity) for x in early] + [(x, 0, cuts[1]) for x in late],
         [(x, cuts[1], capacity) for x in late] + [(x, cuts[2], capacity) for x in near],
     )
@@ -144,10 +145,13 @@
             copy.start()
             page_copies.append(copy)
 
-    for x in early + near:
+    for x in early:
         pack(ctx ^ x)
     pl.semaphore_wait(barrier, greeted)
     send_pages(0)
+    for x in near:
+        pack(ctx ^ x)
+    send_pages(1)
     for x in late:
         pack(ctx ^ x)
     pack(ctx)
@@ -377,7 +381,7 @@
             for copy in z_copies(x):
                 copy.start()
         if_owner(ctx ^ x, start)
-    send_pages(1)
+    send_pages(2)
 
     def finish():
         for x in range(1, n_ctx):
@@ -398,7 +402,7 @@
             forward(0, b, False).start()
 
     if_owner(ctx, finish)
-    send_pages(2)
+    send_pages(3)
     for x in range(1, n_ctx):
         def passed_on(x=x):
             out_copy(x, True).wait_recv()

time: 63.9 us -> 63.7 us (level)
  no operation moved by 1% of the time
where the time goes in v4:
time: 63.7 us; the launch traced here: 63.5 us
  Pallas kernels  62.9 us (99%)
  between operations  0.64 us (1%)
    pallas_call x1, Pallas kernels, on_device(): pl.pallas_call(functools.partial(kernel, n_ctx, n_hd, n_pf, capacity), ou...  59.7 us
    pallas_call x1, Pallas kernels, on_device(): pl.pallas_call(functools.partial(deliver, local_heads), out_shape=(jax.Sh...  3.16 us

profile of v4, /device:TPU:8, one launch (start us, length us, event | category | flops | bytes accessed | tf_op | source)
XLA Modules:
  0.0 63.5 jit_solution(1708526059345992527)
XLA Ops:
  0.6 59.7 %shard_map.95 = (bf16[144,16,512]{2,1,0:T(8,128)(2,1)}, bf16[2,4,64,128]{3,2,1,0:T(8,128)(2,1)}) custom-call(bf16[16,8,16,512]{3,2,1,0:T(8,128)(2,1)} %pages_h.1, s32[8,1,256]{2,1,0:T(1,128)} %bitcast.2, s32[8,256]{1,0:T(8,128)} %bitcast.3, s32[8]{0:T(128)} %lengths_h.1, bf16[2,8,4096]{2,1,0:T(8,128)(2,1)} %queries_h.1, bf16[256,1024]{1,0:T(8,128)(2,1)} %key_up_h.1, ...), custom_call_target="tpu_custom_call" | custom-call | tf_op jit(solution)/shard_map/pallas_call | solution.py:486
  60.3 3.2 %shard_map.96 = (bf16[144,16,512]{2,1,0:T(8,128)(2,1)}, bf16[2,8,4096]{2,1,0:T(8,128)(2,1)}) custom-call(bf16[144,16,512]{2,1,0:T(8,128)(2,1)} %get-tuple-element.6.stored_in, bf16[2,4,64,128]{3,2,1,0:T(8,128)(2,1)} %get-tuple-element.7.rows_in), custom_call_target="tpu_custom_call" | custom-call | tf_op jit(solution)/shard_map/pallas_call | solution.py:523
